TPU v7x, 32 devices: a whole 2x2x4 slice. The times are simulated.
32 devices in a mesh: dp: 4 (over x, core), sp: 8 (over z, y).
Axes of the slice: x: 2, y: 2, z: 4, core: 2. Of those that a mesh axis runs over, the one named last changes fastest.
Arguments:
- frames_in: bfloat16 [2048, 64, 256], P(('dp', 'sp')), may hold values from -6 to 6
- spatial_weight: bfloat16 [3, 3, 256, 256], replicated, may hold values from -0.125 to 0.125
- temporal_weight: bfloat16 [3, 256, 256], replicated, may hold values from -0.21875 to 0.21875
- cotangent: bfloat16 [2048, 64, 256], P(('dp', 'sp')), may hold values from -6 to 6
Outputs:
- block_out: bfloat16 [2048, 64, 256], P(('dp', 'sp'))
- grad_input: bfloat16 [2048, 64, 256], P(('dp', 'sp'))
- grad_spatial: float32 [3, 3, 256, 256], replicated
- grad_temporal: float32 [3, 256, 256], replicated
All inputs are finite; a program needn't handle non-finite values.
Results may differ from a plain program's by a relative error of at most 0.0049.
Values may be sent and summed in bfloat16 or wider, within the bound.
A program may use at most 128 MiB of HBM per device.

v0:
```python
import math
import jax
import jax.numpy as jnp
from jax import lax
from jax.sharding import PartitionSpec as P

H = 64
FRAMES = 4


def contract_rows(left, right):
    return lax.dot_general(
        left, right, (((0,), (0,)), ((), ())), preferred_element_type=jnp.float32
    )


def times_transpose(left, weight):
    return lax.dot_general(
        left, weight, (((1,), (1,)), ((), ())), preferred_element_type=jnp.float32
    )


def local(frames_in, spatial_weight, temporal_weight, cotangent):
    slab_rows, width_cells, channels = frames_in.shape
    sp_count = lax.axis_size("sp")

    def padded_rows(values):
        return jnp.pad(values, ((1, 1), (1, 1), (0, 0)))

    def flatten_rows(values):
        return values.reshape(-1, channels)

    padded_in = padded_rows(frames_in)
    pre = jnp.zeros((slab_rows * width_cells, channels), jnp.float32)
    for tap_row in range(3):
        for tap_col in range(3):
            window = flatten_rows(
                padded_in[tap_row : tap_row + slab_rows, tap_col : tap_col + width_cells]
            )
            pre = pre + jnp.dot(
                window, spatial_weight[tap_row, tap_col], preferred_element_type=jnp.float32
            )
    act = jax.nn.silu(pre).astype(jnp.bfloat16).reshape(slab_rows, width_cells, channels)

    def to_frames(values):
        return lax.all_to_all(values, "sp", split_axis=0, concat_axis=1, tiled=True)

    moved_act, moved_cot = (
        lax.all_to_all(act, "sp", split_axis=1, concat_axis=0, tiled=True),
        lax.all_to_all(cotangent, "sp", split_axis=1, concat_axis=0, tiled=True),
    )
    group_rows = slab_rows * sp_count
    stripe = width_cells // sp_count
    groups = group_rows // (FRAMES * H)
    act_clips = moved_act.reshape(groups, FRAMES, H * stripe, channels)
    cot_clips = moved_cot.reshape(groups, FRAMES, H * stripe, channels)
    act_padded = jnp.pad(act_clips, ((0, 0), (2, 0), (0, 0), (0, 0)))
    cot_padded = jnp.pad(cot_clips, ((0, 0), (0, 2), (0, 0), (0, 0)))
    temporal_sum = jnp.zeros(act_clips.shape, jnp.float32)
    act_grad_sum = jnp.zeros(act_clips.shape, jnp.float32)
    temporal_terms = []
    for tap_step in range(3):
        earlier = act_padded[:, 2 - tap_step : 2 - tap_step + FRAMES]
        temporal_sum = temporal_sum + jnp.einsum(
            "gfpc,cd->gfpd", earlier, temporal_weight[tap_step], preferred_element_type=jnp.float32
        )
        temporal_terms.append(
            jnp.einsum("gfpc,gfpd->cd", earlier, cot_clips, preferred_element_type=jnp.float32)
        )
        later = cot_padded[:, tap_step : tap_step + FRAMES]
        act_grad_sum = act_grad_sum + jnp.einsum(
            "gfpd,cd->gfpc", later, temporal_weight[tap_step], preferred_element_type=jnp.float32
        )
    temporal_out = to_frames(
        temporal_sum.astype(jnp.bfloat16).reshape(group_rows, stripe, channels)
    )
    grad_act = to_frames(act_grad_sum.astype(jnp.bfloat16).reshape(group_rows, stripe, channels))
    grad_temporal = jnp.stack(temporal_terms)
    grad_scale = 1.0 / math.sqrt(slab_rows * sp_count * lax.axis_size("dp") * width_cells)
    block_out = (frames_in.astype(jnp.float32) + temporal_out.astype(jnp.float32)).astype(
        jnp.bfloat16
    )
    sigma = jax.nn.sigmoid(pre)
    grad_pre = (
        flatten_rows(grad_act).astype(jnp.float32) * (sigma * (1.0 + pre * (1.0 - sigma)))
    ).astype(jnp.bfloat16)
    grad_padded = padded_rows(grad_pre.reshape(slab_rows, width_cells, channels))
    spatial_terms = []
    grad_in = flatten_rows(cotangent).astype(jnp.float32)
    for tap_row in range(3):
        for tap_col in range(3):
            window = flatten_rows(
                padded_in[tap_row : tap_row + slab_rows, tap_col : tap_col + width_cells]
            )
            spatial_terms.append(contract_rows(window, grad_pre))
            back_window = flatten_rows(
                grad_padded[
                    2 - tap_row : 2 - tap_row + slab_rows, 2 - tap_col : 2 - tap_col + width_cells
                ]
            )
            grad_in = grad_in + times_transpose(back_window, spatial_weight[tap_row, tap_col])
    grad_spatial = jnp.stack(spatial_terms).reshape(3, 3, channels, channels)
    grad_spatial, grad_temporal = lax.psum((grad_spatial, grad_temporal), ("dp", "sp"))
    grad_input = grad_in.astype(jnp.bfloat16).reshape(slab_rows, width_cells, channels)
    return (block_out, grad_input, grad_spatial * grad_scale, grad_temporal * grad_scale)


def solution(mesh):
    placed = (P(("dp", "sp"), None, None), P(), P(), P(("dp", "sp"), None, None))
    return jax.shard_map(
        local,
        mesh=mesh,
        in_specs=placed,
        out_specs=(P(("dp", "sp"), None, None), P(("dp", "sp"), None, None), P(), P()),
        check_vma=False,
    )
```

profile of v0, /device:TPU:0, one launch (start us, length us, event | category | flops | bytes accessed | tf_op | source)
XLA Modules:
  0.0 385.7 jit_solution(17746489602125472998)
XLA Ops:
  7.2 4.1 %copy.32 = bf16[64,64,256]{2,0,1:T(8,128)(2,1)} copy(bf16[64,64,256]{2,1,0:T(8,128)(2,1)} %param.7) | data formatting | bytes 4194304 | tf_op args[3]
  11.3 7.4 %all-to-all-start.2 = ((bf16[64,64,256]{2,0,1:T(8,128)(2,1)}), bf16[64,64,256]{2,0,1:T(8,128)(2,1)}, u32[]{:S(2)}, u32[]{:S(2)}) async-start(bf16[64,64,256]{2,0,1:T(8,128)(2,1)} %copy.32), calls=%async_computation.2 | async-start | bytes 4194304 | tf_op jit(solution)/shard_map/all_to_all | solution.py:50
  18.7 9.8 %pad_slice_fusion.10 = (bf16[64,64,256]{2,1,0:T(8,128)(2,1)}, bf16[64,64,256]{2,1,0:T(8,128)(2,1)}, bf16[64,64,256]{2,1,0:T(8,128)(2,1)}, bf16[64,64,256]{2,1,0:...) fusion(bf16[64,64,256]{2,1,0:T(8,128)(2,1)S(1)} %copy-done.3), kind=kLoop, calls=%fused_computation.46 | loop fusion | bytes 18874368 | tf_op jit(solution)/shard_map/slice | solution.py:38
  28.4 38.6 %all-to-all-done.2 = bf16[64,64,256]{2,0,1:T(8,128)(2,1)} async-done(((bf16[64,64,256]{2,0,1:T(8,128)(2,1)}), bf16[64,64,256]{2,0,1:T(8,128)(2,1)}, u32[]{:S(2)}, u32[]{:S(2)}) %all-to-all-start.2) | async-done | bytes 2097184 | tf_op jit(solution)/shard_map/all_to_all | solution.py:50
  67.0 2.9 copy.33
  71.4 2.1 add_convert_fusion
  73.5 4.8 %all-to-all-start.3 = ((bf16[512,8,256]{2,1,0:T(8,128)(2,1)}), bf16[512,8,256]{2,1,0:T(8,128)(2,1)}, u32[]{:S(2)}, u32[]{:S(2)}) async-start(bf16[512,8,256]{2,1,0:T(8,128)(2,1)} %bitcast.239), calls=%async_computation.3 | async-start | bytes 4194304 | tf_op jit(solution)/shard_map/all_to_all | solution.py:46
  78.3 2.4 fusion.63
  81.5 0.9 copy-done.16
  83.1 0.9 copy-done.13
  84.7 0.8 convolution_add_fusion.13
  85.5 0.8 copy-done.10
  87.0 0.9 copy-done.8
  88.6 0.9 copy-done.6
  89.4 2.7 convolution_add_fusion.10
  92.1 34.0 %all-to-all-done.3 = bf16[512,8,256]{2,1,0:T(8,128)(2,1)} async-done(((bf16[512,8,256]{2,1,0:T(8,128)(2,1)}), bf16[512,8,256]{2,1,0:T(8,128)(2,1)}, u32[]{:S(2)}, u32[]{:S(2)}) %all-to-all-start.3) | async-done | bytes 2097184 | tf_op jit(solution)/shard_map/all_to_all | solution.py:46
  126.1 2.0 convert_bitcast_fusion
  128.7 1.6 copy-done.23
  130.9 3.5 fusion.2
  134.4 2.5 copy.29
  137.0 4.9 %all-to-all-start = ((bf16[64,64,256]{2,0,1:T(8,128)(2,1)}), bf16[64,64,256]{2,0,1:T(8,128)(2,1)}, u32[]{:S(2)}, u32[]{:S(2)}) async-start(bf16[64,64,256]{2,0,1:T(8,128)(2,1)} %copy.29), calls=%async_computation | async-start | bytes 4194304 | tf_op jit(solution)/shard_map/all_to_all | solution.py:49
  141.9 3.1 fusion.35
  145.3 0.8 fusion.34
  146.1 0.8 copy-done.17
  146.9 0.8 fusion.33
  147.7 0.8 copy-done.14
  149.3 1.0 fusion.31
  151.7 0.8 copy-done.9
  153.3 0.8 copy-done.7
  154.9 0.8 copy-done.26
  156.4 1.4 copy-done.24
  157.8 10.4 %pad_slice_fusion.2 = (bf16[64,64,256]{2,1,0:T(8,128)(2,1)}, bf16[64,64,256]{2,1,0:T(8,128)(2,1)S(1)}, bf16[64,64,256]{2,1,0:T(8,128)(2,1)S(1)}, bf16[64,64,256]...) fusion(bf16[64,64,256]{2,1,0:T(8,128)(2,1)S(1)} %bitcast.256), kind=kLoop, calls=%fused_computation.38 | loop fusion | bytes 18874368 | tf_op jit(solution)/shard_map/slice | solution.py:97
  168.3 0.8 convolution_add_fusion.8
  171.3 2.8 convolution_add_fusion.4
  174.1 15.5 %all-to-all-done = bf16[64,64,256]{2,0,1:T(8,128)(2,1)} async-done(((bf16[64,64,256]{2,0,1:T(8,128)(2,1)}), bf16[64,64,256]{2,0,1:T(8,128)(2,1)}, u32[]{:S(2)}, u32[]{:S(2)}) %all-to-all-start) | async-done | bytes 2097184 | tf_op jit(solution)/shard_map/all_to_all | solution.py:49
  189.6 3.0 copy.30
  195.1 2.0 add_convert_fusion.1
  197.1 4.4 %all-to-all-start.1 = ((bf16[512,8,256]{2,1,0:T(8,128)(2,1)}), bf16[512,8,256]{2,1,0:T(8,128)(2,1)}, u32[]{:S(2)}, u32[]{:S(2)}) async-start(bf16[512,8,256]{2,1,0:T(8,128)(2,1)} %bitcast.238), calls=%async_computation.1 | async-start | bytes 4194304 | tf_op jit(solution)/shard_map/all_to_all | solution.py:46
  202.0 1.3 copy-done.2
  204.8 0.9 pad_maximum_fusion
  205.8 3.7 convolution_add_fusion.3
  209.5 0.8 convolution_add_fusion.2
  211.8 0.8 copy-done.12
  212.7 2.1 fusion
  214.8 154.8 %all-reduce.7.cloned.1.call-done = (f32[3,3,256,256]{3,2,1,0:T(8,128)}, f32[3,256,256]{2,1,0:T(8,128)}) async-done(((f32[3,3,256,256]{3,2,1,0:T(8,128)}, f32[3,256,256]{2,1,0:T(8,128)}), (f32[3,3,256,256]{3,2,1,0:T(8,128)}, f32[3,256,256]{2,1,0:T(8,128)})) %all-reduce.7.cloned.1.call-update) | async-done | bytes 3145744 | tf_op jit(solution)/shard_map/psum | solution.py:103
  369.6 2.1 broadcast_multiply_fusion.1
  371.6 3.4 broadcast_multiply_fusion
  375.1 3.6 fusion.1
  (70 shorter events, 19.3 us)
Async XLA Ops:
  11.2 7.4 %copy-start.3 = (bf16[64,64,256]{2,1,0:T(8,128)(2,1)S(1)}, bf16[64,64,256]{2,1,0:T(8,128)(2,1)}, u32[]{:S(2)}) copy-start(bf16[64,64,256]{2,1,0:T(8,128)(2,1)} %param.4) | copy-start | bytes 6291460
  11.3 55.8 %all-to-all-start.2 = ((bf16[64,64,256]{2,0,1:T(8,128)(2,1)}), bf16[64,64,256]{2,0,1:T(8,128)(2,1)}, u32[]{:S(2)}, u32[]{:S(2)}) async-start(bf16[64,64,256]{2,0,1:T(8,128)(2,1)} %copy.32), calls=%async_computation.2 | async-start | bytes 4194304 | tf_op jit(solution)/shard_map/all_to_all | solution.py:50
  67.0 2.9 copy-start.27
  69.9 1.5 copy-start
  73.5 4.8 %copy-start.22 = (bf16[3,3,256,256]{3,2,1,0:T(8,128)(2,1)S(1)}, bf16[3,3,256,256]{3,2,1,0:T(8,128)(2,1)}, u32[]{:S(2)}) copy-start(bf16[3,3,256,256]{3,2,1,0:T(8,128)(2,1)} %param.5) | copy-start | bytes 3538948
  73.5 52.6 %all-to-all-start.3 = ((bf16[512,8,256]{2,1,0:T(8,128)(2,1)}), bf16[512,8,256]{2,1,0:T(8,128)(2,1)}, u32[]{:S(2)}, u32[]{:S(2)}) async-start(bf16[512,8,256]{2,1,0:T(8,128)(2,1)} %bitcast.239), calls=%async_computation.3 | async-start | bytes 4194304 | tf_op jit(solution)/shard_map/all_to_all | solution.py:46
  78.3 2.5 copy-start.19
  80.8 1.6 copy-start.16
  82.4 1.6 copy-start.13
  84.7 1.6 copy-start.10
  86.3 1.6 copy-start.8
  87.8 1.6 copy-start.6
  128.1 2.2 copy-start.23
  128.1 2.9 copy-start.25
  137.0 52.7 %all-to-all-start = ((bf16[64,64,256]{2,0,1:T(8,128)(2,1)}), bf16[64,64,256]{2,0,1:T(8,128)(2,1)}, u32[]{:S(2)}, u32[]{:S(2)}) async-start(bf16[64,64,256]{2,0,1:T(8,128)(2,1)} %copy.29), calls=%async_computation | async-start | bytes 4194304 | tf_op jit(solution)/shard_map/all_to_all | solution.py:49
  141.9 3.1 copy-start.20
  141.9 3.5 copy-start.21
  145.3 1.6 copy-start.17
  146.9 1.6 copy-start.14
  149.3 1.6 copy-start.11
  150.9 1.6 copy-start.9
  152.5 1.6 copy-start.7
  154.1 1.6 copy-start.26
  156.4 1.4 copy-start.24
  157.8 10.5 %copy-start.5 = (bf16[64,64,256]{2,1,0:T(8,128)(2,1)S(1)}, bf16[64,64,256]{2,1,0:T(8,128)(2,1)}, u32[]{:S(2)}) copy-start(bf16[64,64,256]{2,1,0:T(8,128)(2,1)} %param.7) | copy-start | bytes 6291460
  189.6 3.0 copy-start.1
  192.7 1.0 copy-start.28
  197.1 178.0 %all-to-all-start.1 = ((bf16[512,8,256]{2,1,0:T(8,128)(2,1)}), bf16[512,8,256]{2,1,0:T(8,128)(2,1)}, u32[]{:S(2)}, u32[]{:S(2)}) async-start(bf16[512,8,256]{2,1,0:T(8,128)(2,1)} %bitcast.238), calls=%async_computation.1 | async-start | bytes 4194304 | tf_op jit(solution)/shard_map/all_to_all | solution.py:46
  201.5 168.1 %all-reduce.7.cloned.1.call-start = ((), (), s32[]{:S(2)}) async-start(), calls=%async_computation.4 | async-start | bytes 6291456 | tf_op jit(solution)/shard_map/psum | solution.py:103
  201.7 1.6 copy-start.2
  205.8 3.7 copy-start.18
  209.5 1.6 copy-start.15
  211.1 1.6 copy-start.12
  371.6 3.4 copy-start.4
Sparse Core Ops, SparseCore 0:
  208.5 160.9 all-reduce.6
where the time goes:
time: 393 us; the launch traced here: 386 us
  waiting for transfers between devices  243 us (62%)
  local copies, waits for them, and re-layouts  49.7 us (13%)
  matrix products  44.8 us (11%)
  starting transfers between devices  21.7 us (6%)
  between operations  14.7 us (4%)
  other arithmetic  12 us (3%)
    psum x1, waiting for transfers between devices, local(): lax.psum((grad_spatial, grad_temporal), ('dp', 'sp'))  155 us
    all_to_all x1, waiting for transfers between devices, local(): lax.all_to_all(cotangent, 'sp', split_axis=1, concat_axis=0, tiled=True)  38.6 us
    all_to_all x2, waiting for transfers between devices, to_frames(): return lax.all_to_all(values, 'sp', split_axis=0, concat_axis=1, tiled=True)  34 us
    unnamed x59, local copies, waits for them, and re-layouts  20.2 us
    all_to_all x1, waiting for transfers between devices, local(): lax.all_to_all(act, 'sp', split_axis=1, concat_axis=0, tiled=True)  15.5 us
    dot_general x9, matrix products, times_transpose(): lax.dot_general(left, weight, (((1,), (1,)), ((), ())), preferred_element...  13.1 us
    dot_general x9, matrix products, local(): jnp.dot(window, spatial_weight[tap_row, tap_col], preferred_element_type=...  13 us
    slice x1, local copies, waits for them, and re-layouts, local(): grad_padded[2 - tap_row:2 - tap_row + slab_rows, 2 - tap_col:2 - tap_col...  10.4 us
  transfers between devices with their start and end apart: 5, of which 4 were waited for; matrix products, arithmetic and copies ran while one was open for 16% of the time, Pallas kernels for 0%

commit v1 on v0

--- a/solution.py
+++ b/solution.py
@@ -6,6 +6,22 @@
 
 H = 64
 FRAMES = 4
+
+
+def swapped_with_each(x, axis, split, join):
+    ways, here = (lax.axis_size(axis), lax.axis_index(axis))
+    width = x.shape[split] // ways
+    lengths = list(x.shape)
+    lengths[split] = width
+    height = lengths[join]
+    lengths[join] = height * ways
+    full = jnp.zeros(lengths, x.dtype)
+    for mask in range(ways):
+        part = lax.dynamic_slice_in_dim(x, (here ^ mask) * width, width, axis=split)
+        if mask:
+            part = lax.ppermute(part, axis, [(d, d ^ mask) for d in range(ways)])
+        full = lax.dynamic_update_slice_in_dim(full, part, (here ^ mask) * height, axis=join)
+    return full
 
 
 def contract_rows(left, right):
@@ -47,7 +63,7 @@
 
     moved_act, moved_cot = (
         lax.all_to_all(act, "sp", split_axis=1, concat_axis=0, tiled=True),
-        lax.all_to_all(cotangent, "sp", split_axis=1, concat_axis=0, tiled=True),
+        swapped_with_each(cotangent, "sp", 1, 0),
     )
     group_rows = slab_rows * sp_count
     stripe = width_cells // sp_count

time: 393 us -> 386 us (0.982)
  waiting for transfers between devices: 243 us -> 221 us
  starting transfers between devices: 21.7 us -> 36.5 us
    all_to_all x1 -> x0, waiting for transfers between devices: 38.6 us -> none  [local(): lax.all_to_all(cotangent, 'sp', split_axis=1, concat_axis=0, tiled=True)]
    ppermute x0 -> x7, starting transfers between devices: none -> 21 us  [swapped_with_each(): part = lax.ppermute(part, axis, [(d, d ^ mask) for d in range(ways)])]
    ppermute x0 -> x7, waiting for transfers between devices: none -> 17.5 us  [swapped_with_each(): part = lax.ppermute(part, axis, [(d, d ^ mask) for d in range(ways)])]
    all_to_all x1 -> x0, starting transfers between devices: 7.41 us -> none  [local(): lax.all_to_all(cotangent, 'sp', split_axis=1, concat_axis=0, tiled=True)]
    dynamic_update_slice x0 -> x7, local copies, waits for them, and re-layouts: none -> 4.9 us  [swapped_with_each(): lax.dynamic_update_slice_in_dim(full, part, (here ^ mask) * height, axis=...]
    unnamed x59 -> x66, local copies, waits for them, and re-layouts: 20.2 us -> 20.3 us
  transfers between devices with their start and end apart: 5 -> 11, of which waited for: 4 -> 5; matrix products, arithmetic and copies ran while one was open for 16% -> 16% of each run, Pallas kernels for 0% -> 0%
where the time goes in v1:
time: 386 us; the launch traced here: 380 us
  waiting for transfers between devices  221 us (57%)
  local copies, waits for them, and re-layouts  53 us (14%)
  matrix products  42.2 us (11%)
  starting transfers between devices  36.5 us (9%)
  between operations  14.8 us (4%)
  other arithmetic  11.9 us (3%)
    psum x1, waiting for transfers between devices, local(): lax.psum((grad_spatial, grad_temporal), ('dp', 'sp'))  154 us
    all_to_all x2, waiting for transfers between devices, to_frames(): return lax.all_to_all(values, 'sp', split_axis=0, concat_axis=1, tiled=True)  33.7 us
    ppermute x7, starting transfers between devices, swapped_with_each(): part = lax.ppermute(part, axis, [(d, d ^ mask) for d in range(ways)])  21 us
    unnamed x66, local copies, waits for them, and re-layouts  20.3 us
    ppermute x7, waiting for transfers between devices, swapped_with_each(): part = lax.ppermute(part, axis, [(d, d ^ mask) for d in range(ways)])  17.5 us
    all_to_all x1, waiting for transfers between devices, local(): lax.all_to_all(act, 'sp', split_axis=1, concat_axis=0, tiled=True)  15.6 us
    dot_general x9, matrix products, times_transpose(): lax.dot_general(left, weight, (((1,), (1,)), ((), ())), preferred_element...  12.4 us
    dot_general x9, matrix products, local(): jnp.dot(window, spatial_weight[tap_row, tap_col], preferred_element_type=...  11.1 us
  transfers between devices with their start and end apart: 11, of which 5 were waited for; matrix products, arithmetic and copies ran while one was open for 16% of the time, Pallas kernels for 0%

profile of v1, /device:TPU:0, one launch (start us, length us, event | category | flops | bytes accessed | tf_op | source)
XLA Modules:
  0.0 379.5 jit_solution(8084926303365813939)
XLA Ops:
  7.4 1.4 copy-done.6
  8.8 1.1 constant_dynamic-slice_fusion
  9.9 6.0 %collective-permute-start.6 = (bf16[64,8,256]{2,1,0:T(8,128)(2,1)S(1)}, bf16[64,8,256]{2,1,0:T(8,128)(2,1)}, u32[]{:S(2)}, u32[]{:S(2)}) collective-permute-start(bf16[64,8,256]{2,1,0:T(8,128)(2,1)S(1)} %get-tuple-element.18), channel_id=1, source_target_pairs={{0,7},{1,6},{2,5},{3,4},{4,3},{5,2},{6,1},{7,0},{8,15},{9,14},{10,... | collective-permute-start | bytes 786440 | tf_op jit(solution)/shard_map/ppermute | solution.py:22
  15.9 1.7 collective-permute-start.2
  18.2 1.1 collective-permute-start
  19.4 9.8 %pad_slice_fusion.10 = (bf16[64,64,256]{2,1,0:T(8,128)(2,1)}, bf16[64,64,256]{2,1,0:T(8,128)(2,1)}, bf16[64,64,256]{2,1,0:T(8,128)(2,1)}, bf16[64,64,256]{2,1,0:...) fusion(bf16[64,64,256]{2,1,0:T(8,128)(2,1)S(1)} %copy-done.3), kind=kLoop, calls=%fused_computation.46 | loop fusion | bytes 18874368 | tf_op jit(solution)/shard_map/slice | solution.py:54
  29.2 4.5 %collective-permute-done = bf16[64,8,256]{2,1,0:T(8,128)(2,1)} collective-permute-done((bf16[64,8,256]{2,1,0:T(8,128)(2,1)}, bf16[64,8,256]{2,1,0:T(8,128)(2,1)}, u32[]{:S(2)}, u32[]{:S(2)}) %collective-permute-start) | collective-permute-done | bytes 262176 | tf_op jit(solution)/shard_map/ppermute | solution.py:22
  33.6 10.1 %collective-permute-start.3 = (bf16[64,8,256]{2,1,0:T(8,128)(2,1)S(1)}, bf16[64,8,256]{2,1,0:T(8,128)(2,1)S(1)}, u32[]{:S(2)}, u32[]{:S(2)}) collective-permute-start(bf16[64,8,256]{2,1,0:T(8,128)(2,1)S(1)} %get-tuple-element.20), channel_id=1, source_target_pairs={{0,4},{1,5},{2,6},{3,7},{4,0},{5,1},{6,2},{7,3},{8,12},{9,13},{10,... | collective-permute-start | bytes 786440 | tf_op jit(solution)/shard_map/ppermute | solution.py:22
  43.8 1.0 constant_dynamic-update-slice_fusion.5
  44.7 1.3 collective-permute-start.5
  46.1 1.0 constant_dynamic-update-slice_fusion.4
  47.1 1.0 constant_dynamic-update-slice_fusion.3
  48.0 13.1 %collective-permute-done.3 = bf16[64,8,256]{2,1,0:T(8,128)(2,1)S(1)} collective-permute-done((bf16[64,8,256]{2,1,0:T(8,128)(2,1)S(1)}, bf16[64,8,256]{2,1,0:T(8,128)(2,1)S(1)}, u32[]{:S(2)}, u32[]{:S(2)}) %collective-permute-start.3) | collective-permute-done | bytes 262176 | tf_op jit(solution)/shard_map/ppermute | solution.py:22
  61.1 1.0 constant_dynamic-update-slice_fusion.1
  62.2 1.0 constant_dynamic-update-slice_fusion.6
  64.7 2.1 add_convert_fusion
  66.7 6.0 %all-to-all-start.2 = ((bf16[512,8,256]{2,1,0:T(8,128)(2,1)}), bf16[512,8,256]{2,1,0:T(8,128)(2,1)}, u32[]{:S(2)}, u32[]{:S(2)}) async-start(bf16[512,8,256]{2,1,0:T(8,128)(2,1)} %bitcast.238), calls=%async_computation.2 | async-start | bytes 4194304 | tf_op jit(solution)/shard_map/all_to_all | solution.py:62
  73.5 0.9 copy-done.19
  75.1 0.9 copy-done.17
  76.7 0.9 copy-done.15
  78.3 0.9 copy-done.4
  81.5 0.9 copy-done.11
  83.1 0.9 copy-done.9
  83.9 2.7 convolution_add_fusion.10
  86.6 33.7 %all-to-all-done.2 = bf16[512,8,256]{2,1,0:T(8,128)(2,1)} async-done(((bf16[512,8,256]{2,1,0:T(8,128)(2,1)}), bf16[512,8,256]{2,1,0:T(8,128)(2,1)}, u32[]{:S(2)}, u32[]{:S(2)}) %all-to-all-start.2) | async-done | bytes 2097184 | tf_op jit(solution)/shard_map/all_to_all | solution.py:62
  120.3 2.0 convert_bitcast_fusion
  122.9 1.6 copy-done.27
  125.2 3.5 fusion.2
  128.6 2.5 copy.27
  131.1 4.9 %all-to-all-start = ((bf16[64,64,256]{2,0,1:T(8,128)(2,1)}), bf16[64,64,256]{2,0,1:T(8,128)(2,1)}, u32[]{:S(2)}, u32[]{:S(2)}) async-start(bf16[64,64,256]{2,0,1:T(8,128)(2,1)} %copy.27), calls=%async_computation | async-start | bytes 4194304 | tf_op jit(solution)/shard_map/all_to_all | solution.py:65
  136.1 3.1 fusion.35
  143.5 1.0 fusion.31
  150.6 1.4 copy-done.28
  152.0 10.4 %pad_slice_fusion.2 = (bf16[64,64,256]{2,1,0:T(8,128)(2,1)}, bf16[64,64,256]{2,1,0:T(8,128)(2,1)S(1)}, bf16[64,64,256]{2,1,0:T(8,128)(2,1)S(1)}, bf16[64,64,256]...) fusion(bf16[64,64,256]{2,1,0:T(8,128)(2,1)S(1)} %bitcast.255), kind=kLoop, calls=%fused_computation.38 | loop fusion | bytes 18874368 | tf_op jit(solution)/shard_map/slice | solution.py:113
  165.5 2.8 convolution_add_fusion.4
  168.3 15.6 %all-to-all-done = bf16[64,64,256]{2,0,1:T(8,128)(2,1)} async-done(((bf16[64,64,256]{2,0,1:T(8,128)(2,1)}), bf16[64,64,256]{2,0,1:T(8,128)(2,1)}, u32[]{:S(2)}, u32[]{:S(2)}) %all-to-all-start) | async-done | bytes 2097184 | tf_op jit(solution)/shard_map/all_to_all | solution.py:65
  183.9 3.0 copy.28
  189.3 2.0 add_convert_fusion.1
  191.3 4.4 %all-to-all-start.1 = ((bf16[512,8,256]{2,1,0:T(8,128)(2,1)}), bf16[512,8,256]{2,1,0:T(8,128)(2,1)}, u32[]{:S(2)}, u32[]{:S(2)}) async-start(bf16[512,8,256]{2,1,0:T(8,128)(2,1)} %bitcast.237), calls=%async_computation.1 | async-start | bytes 4194304 | tf_op jit(solution)/shard_map/all_to_all | solution.py:62
  196.3 1.3 copy-done.2
  199.0 0.9 pad_maximum_fusion
  200.0 0.9 copy-done.24
  200.9 3.1 convolution_add_fusion.3
  207.2 2.1 fusion
  209.2 154.2 %all-reduce.7.cloned.1.call-done = (f32[3,3,256,256]{3,2,1,0:T(8,128)}, f32[3,256,256]{2,1,0:T(8,128)}) async-done(((f32[3,3,256,256]{3,2,1,0:T(8,128)}, f32[3,256,256]{2,1,0:T(8,128)}), (f32[3,3,256,256]{3,2,1,0:T(8,128)}, f32[3,256,256]{2,1,0:T(8,128)})) %all-reduce.7.cloned.1.call-update) | async-done | bytes 3145744 | tf_op jit(solution)/shard_map/psum | solution.py:119
  363.5 2.1 broadcast_multiply_fusion.1
  365.5 3.4 broadcast_multiply_fusion
  369.0 3.5 fusion.1
  (97 shorter events, 30.4 us)
Async XLA Ops:
  7.2 1.6 copy-start.6
  8.8 10.6 %copy-start.3 = (bf16[64,64,256]{2,1,0:T(8,128)(2,1)S(1)}, bf16[64,64,256]{2,1,0:T(8,128)(2,1)}, u32[]{:S(2)}) copy-start(bf16[64,64,256]{2,1,0:T(8,128)(2,1)} %param.4) | copy-start | bytes 6291460
  9.9 52.3 %collective-permute-start.6 = (bf16[64,8,256]{2,1,0:T(8,128)(2,1)S(1)}, bf16[64,8,256]{2,1,0:T(8,128)(2,1)}, u32[]{:S(2)}, u32[]{:S(2)}) collective-permute-start(bf16[64,8,256]{2,1,0:T(8,128)(2,1)S(1)} %get-tuple-element.18), channel_id=1, source_target_pairs={{0,7},{1,6},{2,5},{3,4},{4,3},{5,2},{6,1},{7,0},{8,15},{9,14},{10,... | collective-permute-start | bytes 786440 | tf_op jit(solution)/shard_map/ppermute | solution.py:22
  15.9 45.3 %collective-permute-start.4 = (bf16[64,8,256]{2,1,0:T(8,128)(2,1)S(1)}, bf16[64,8,256]{2,1,0:T(8,128)(2,1)}, u32[]{:S(2)}, u32[]{:S(2)}) collective-permute-start(bf16[64,8,256]{2,1,0:T(8,128)(2,1)S(1)} %get-tuple-element.19), channel_id=1, source_target_pairs={{0,5},{1,4},{2,7},{3,6},{4,1},{5,0},{6,3},{7,2},{8,13},{9,12},{10,... | collective-permute-start | bytes 786440 | tf_op jit(solution)/shard_map/ppermute | solution.py:22
  15.9 31.2 %collective-permute-start.2 = (bf16[64,8,256]{2,1,0:T(8,128)(2,1)}, bf16[64,8,256]{2,1,0:T(8,128)(2,1)}, u32[]{:S(2)}, u32[]{:S(2)}) collective-permute-start(bf16[64,8,256]{2,1,0:T(8,128)(2,1)} %get-tuple-element.21), channel_id=1, source_target_pairs={{0,3},{1,2},{2,1},{3,0},{4,7},{5,6},{6,5},{7,4},{8,11},{9,10},{10,... | collective-permute-start | bytes 786440 | tf_op jit(solution)/shard_map/ppermute | solution.py:22
  17.6 27.2 %collective-permute-start.1 = (bf16[64,8,256]{2,1,0:T(8,128)(2,1)}, bf16[64,8,256]{2,1,0:T(8,128)(2,1)}, u32[]{:S(2)}, u32[]{:S(2)}) collective-permute-start(bf16[64,8,256]{2,1,0:T(8,128)(2,1)} %get-tuple-element.22), channel_id=1, source_target_pairs={{0,2},{1,3},{2,0},{3,1},{4,6},{5,7},{6,4},{7,5},{8,10},{9,11},{10,... | collective-permute-start | bytes 786440 | tf_op jit(solution)/shard_map/ppermute | solution.py:22
  18.2 15.4 %collective-permute-start = (bf16[64,8,256]{2,1,0:T(8,128)(2,1)}, bf16[64,8,256]{2,1,0:T(8,128)(2,1)}, u32[]{:S(2)}, u32[]{:S(2)}) collective-permute-start(bf16[64,8,256]{2,1,0:T(8,128)(2,1)} %get-tuple-element.23), channel_id=1, source_target_pairs={{0,1},{1,0},{2,3},{3,2},{4,5},{5,4},{6,7},{7,6},{8,9},{9,8},{10,11... | collective-permute-start | bytes 786440 | tf_op jit(solution)/shard_map/ppermute | solution.py:22
  29.2 34.0 %copy-start.31 = (bf16[3,256,256]{2,1,0:T(8,128)(2,1)S(1)}, bf16[3,256,256]{2,1,0:T(8,128)(2,1)}, u32[]{:S(2)}) copy-start(bf16[3,256,256]{2,1,0:T(8,128)(2,1)} %param.6) | copy-start | bytes 1179652
  33.6 27.5 %collective-permute-start.3 = (bf16[64,8,256]{2,1,0:T(8,128)(2,1)S(1)}, bf16[64,8,256]{2,1,0:T(8,128)(2,1)S(1)}, u32[]{:S(2)}, u32[]{:S(2)}) collective-permute-start(bf16[64,8,256]{2,1,0:T(8,128)(2,1)S(1)} %get-tuple-element.20), channel_id=1, source_target_pairs={{0,4},{1,5},{2,6},{3,7},{4,0},{5,1},{6,2},{7,3},{8,12},{9,13},{10,... | collective-permute-start | bytes 786440 | tf_op jit(solution)/shard_map/ppermute | solution.py:22
  44.7 17.4 %collective-permute-start.5 = (bf16[64,8,256]{2,1,0:T(8,128)(2,1)S(1)}, bf16[64,8,256]{2,1,0:T(8,128)(2,1)S(1)}, u32[]{:S(2)}, u32[]{:S(2)}) collective-permute-start(bf16[64,8,256]{2,1,0:T(8,128)(2,1)S(1)} %get-tuple-element.25), channel_id=1, source_target_pairs={{0,6},{1,7},{2,4},{3,5},{4,2},{5,3},{6,0},{7,1},{8,14},{9,15},{10,... | collective-permute-start | bytes 786440 | tf_op jit(solution)/shard_map/ppermute | solution.py:22
  63.1 1.5 copy-start
  66.7 6.1 %copy-start.8 = (bf16[64,64,256]{2,1,0:T(8,128)(2,1)S(1)}, bf16[64,64,256]{2,1,0:T(8,128)(2,1)}, u32[]{:S(2)}) copy-start(bf16[64,64,256]{2,1,0:T(8,128)(2,1)} %get-tuple-element.33) | copy-start | bytes 6291460
  66.7 6.1 %copy-start.26 = (bf16[3,3,256,256]{3,2,1,0:T(8,128)(2,1)S(1)}, bf16[3,3,256,256]{3,2,1,0:T(8,128)(2,1)}, u32[]{:S(2)}) copy-start(bf16[3,3,256,256]{3,2,1,0:T(8,128)(2,1)} %param.5) | copy-start | bytes 3538948
  66.7 53.6 %all-to-all-start.2 = ((bf16[512,8,256]{2,1,0:T(8,128)(2,1)}), bf16[512,8,256]{2,1,0:T(8,128)(2,1)}, u32[]{:S(2)}, u32[]{:S(2)}) async-start(bf16[512,8,256]{2,1,0:T(8,128)(2,1)} %bitcast.238), calls=%async_computation.2 | async-start | bytes 4194304 | tf_op jit(solution)/shard_map/all_to_all | solution.py:62
  72.8 1.6 copy-start.19
  74.4 1.6 copy-start.17
  76.0 1.6 copy-start.15
  77.6 1.6 copy-start.4
  79.2 1.6 copy-start.13
  80.8 1.6 copy-start.11
  82.3 1.6 copy-start.9
  122.3 2.2 copy-start.27
  122.3 2.9 copy-start.29
  131.1 52.7 %all-to-all-start = ((bf16[64,64,256]{2,0,1:T(8,128)(2,1)}), bf16[64,64,256]{2,0,1:T(8,128)(2,1)}, u32[]{:S(2)}, u32[]{:S(2)}) async-start(bf16[64,64,256]{2,0,1:T(8,128)(2,1)} %copy.27), calls=%async_computation | async-start | bytes 4194304 | tf_op jit(solution)/shard_map/all_to_all | solution.py:65
  136.0 3.1 copy-start.20
  136.1 3.5 copy-start.25
  139.5 1.6 copy-start.18
  141.1 1.6 copy-start.16
  143.5 1.6 copy-start.14
  145.1 1.6 copy-start.12
  146.7 1.6 copy-start.10
  148.3 1.6 copy-start.30
  150.6 1.4 copy-start.28
  152.0 10.4 %copy-start.7 = (bf16[64,64,256]{2,1,0:T(8,128)(2,1)S(1)}, bf16[64,64,256]{2,1,0:T(8,128)(2,1)}, u32[]{:S(2)}) copy-start(bf16[64,64,256]{2,1,0:T(8,128)(2,1)} %param.7) | copy-start | bytes 6291460
  183.9 3.0 copy-start.1
  186.9 1.0 copy-start.32
  191.3 177.6 %all-to-all-start.1 = ((bf16[512,8,256]{2,1,0:T(8,128)(2,1)}), bf16[512,8,256]{2,1,0:T(8,128)(2,1)}, u32[]{:S(2)}, u32[]{:S(2)}) async-start(bf16[512,8,256]{2,1,0:T(8,128)(2,1)} %bitcast.237), calls=%async_computation.1 | async-start | bytes 4194304 | tf_op jit(solution)/shard_map/all_to_all | solution.py:62
  195.7 167.8 %all-reduce.7.cloned.1.call-start = ((), (), s32[]{:S(2)}) async-start(), calls=%async_computation.3 | async-start | bytes 6291456 | tf_op jit(solution)/shard_map/psum | solution.py:119
  195.9 1.6 copy-start.2
  199.0 1.9 copy-start.24
  200.9 3.1 copy-start.23
  204.0 1.6 copy-start.22
  205.6 1.6 copy-start.21
  365.5 3.4 copy-start.5
Sparse Core Ops, SparseCore 0:
  202.7 160.6 all-reduce.6
